TPU v7x, 128 devices: a whole 4x4x4 slice. The times are simulated.
128 devices in a mesh: seq: 16 (over x_hi, y, core), head: 8 (over x_lo, z).
Axes of the slice: x: 4 (x_hi: 2, x_lo: 2; x = x_hi * 2 + x_lo), y: 4, z: 4, core: 2. Of those that a mesh axis runs over, the one named last changes fastest.
Arguments:
- lightning_qkv: bfloat16 [8192, 3, 4096], P('seq', None, 'head'), may hold values from -1.796875 to 1.796875
- residual: bfloat16 [8192, 6144], P(('seq', 'head')), may hold values from -6 to 6
- decay_rate: float32 [32], replicated, may hold values from 0 to 1
- lightning_gain: float32 [4096], P('head'), may hold values from 0.1 to 1.9
- out_weight: bfloat16 [4096, 6144], P('head'), may hold values from -0.09375 to 0.09375
- attn_gain: float32 [6144], replicated, may hold values from 0.1 to 1.9
- query_weight: bfloat16 [6144, 4096], P(None, 'head'), may hold values from -3 to 3
- key_value_weight: bfloat16 [6144, 8, 2, 128], P(None, 'head'), may hold values from -1 to 1
- window: int32 [32], replicated, may hold values from 512 to 1024, as said below
Outputs:
- updated: float32 [8192, 6144], P(('seq', 'head'))
- attention: bfloat16 [8192, 4096], P('seq', 'head')
Inputs may be any that keep to these rules, and one draw needn't show every extreme that they name: Query head h at position i sees keys at positions i - window[h] + 1 to i.
All inputs are finite; a program needn't handle non-finite values.
Results may differ from a plain program's by a relative error of at most 0.03.
Values may be sent and summed in bfloat16 or wider, within the bound.
A program may use at most 128 MiB of HBM per device.

v0:
```python
import jax
import jax.numpy as jnp
from jax import lax
from jax.sharding import PartitionSpec as P

HEAD_SIZE = 128


epsilon = 1e-06


def carried_in(value, axis, combine, identity):
    devices, position = (lax.axis_size(axis), lax.axis_index(axis))
    everything = jax.tree.map(lambda part: lax.all_gather(part, axis), value)
    start = jax.tree.map(
        lambda part, zero: jnp.broadcast_to(jnp.asarray(zero, part.dtype), part.shape),
        value,
        identity,
    )

    def hop(k, before):
        reached = k < position
        new = combine(before, jax.tree.map(lambda part: part[k], everything))
        return jax.tree.map(lambda a, b: jnp.where(reached, a, b), new, before)

    return lax.fori_loop(0, devices, hop, start)


def shifted(value, axis, steps):
    count = lax.axis_size(axis)
    leading, last = (max(0, -steps), min(count, count - steps))
    return lax.ppermute(value, axis, [(source, source + steps) for source in range(leading, last)])


def rms_scale(values, gain_vec):
    return (
        values * lax.rsqrt(jnp.mean(values * values, axis=-1, keepdims=True) + epsilon) * gain_vec
    )


def rounded_term(values):
    return lax.optimization_barrier(values.astype(jnp.bfloat16)).astype(jnp.float32)


def on_device(
    lightning_qkv,
    residual,
    decay_rate,
    lightning_gain,
    out_weight,
    attn_gain,
    query_weight,
    key_value_weight,
    window,
):
    tok_rows = lightning_qkv.shape[0]
    heads_here = lightning_gain.shape[0] // HEAD_SIZE
    head_pos = lax.axis_index("head")
    seq_pos = lax.axis_index("seq")
    decays = lax.dynamic_slice_in_dim(decay_rate, head_pos * heads_here, heads_here)
    lin_query = lightning_qkv[:, 0].reshape(tok_rows, heads_here, HEAD_SIZE)
    lin_key = lightning_qkv[:, 1].reshape(tok_rows, heads_here, HEAD_SIZE)
    lin_value = lightning_qkv[:, 2].reshape(tok_rows, heads_here, HEAD_SIZE)
    offsets = jnp.arange(tok_rows)
    spacing = (offsets[:, None] - offsets[None, :]).astype(jnp.float32)
    causal = offsets[:, None] >= offsets[None, :]
    intra_decay = jnp.where(
        causal[None], jnp.exp(-decays[:, None, None] * jnp.maximum(spacing, 0.0)[None]), 0.0
    )
    key_decay = jnp.exp(-decays[None, :] * (tok_rows - 1 - offsets).astype(jnp.float32)[:, None])
    query_decay = jnp.exp(-decays[None, :] * (offsets + 1).astype(jnp.float32)[:, None])
    block_decay = jnp.exp(-decays * tok_rows)
    scores = jnp.einsum("ihd,jhd->hij", lin_query, lin_key, preferred_element_type=jnp.float32)
    weights = (scores * intra_decay).astype(jnp.bfloat16)
    intra_out = jnp.einsum("hij,jhd->ihd", weights, lin_value, preferred_element_type=jnp.float32)
    decayed = (lin_key.astype(jnp.float32) * key_decay[:, :, None]).astype(jnp.bfloat16)
    block_state = jnp.einsum("jhd,jhe->hde", decayed, lin_value, preferred_element_type=jnp.float32)

    def compose(earlier, later):
        return (earlier[0] * later[0], later[0][:, None, None] * earlier[1] + later[1])

    identity = (
        jnp.ones((heads_here,), jnp.float32),
        jnp.zeros((heads_here, HEAD_SIZE, HEAD_SIZE), jnp.float32),
    )
    prefix = carried_in((block_decay, block_state), "seq", compose, identity)
    start_state = prefix[1]
    carried = jnp.einsum(
        "ihd,hde->ihe",
        lin_query.astype(jnp.float32) * query_decay[:, :, None],
        start_state,
        precision=lax.Precision.HIGHEST,
    )
    lightning_out = intra_out + carried
    normed = rms_scale(lightning_out, lightning_gain.reshape(heads_here, HEAD_SIZE)).astype(
        jnp.bfloat16
    )
    normed = normed.reshape(tok_rows, heads_here * HEAD_SIZE)
    kv_flat = key_value_weight.reshape(key_value_weight.shape[0], -1)
    query_cols = query_weight.shape[1]
    summed = lax.psum_scatter(
        rounded_term(jnp.dot(normed, out_weight, preferred_element_type=jnp.float32)).astype(
            jnp.bfloat16
        ),
        "head",
        scatter_dimension=0,
        tiled=True,
    ).astype(jnp.float32)
    updated = residual.astype(jnp.float32) + summed
    prepared_inputs = rms_scale(updated, attn_gain).astype(jnp.bfloat16)
    pieces = lax.all_gather(prepared_inputs, "head", axis=0, tiled=True)
    query_part = jnp.dot(pieces, query_weight, preferred_element_type=jnp.float32)
    key_value_piece = jnp.dot(pieces, kv_flat, preferred_element_type=jnp.float32)
    projected = jnp.concatenate((query_part, key_value_piece), axis=1).astype(jnp.bfloat16)
    kv_heads_here = key_value_weight.shape[1]
    query_group_count = query_cols // HEAD_SIZE // kv_heads_here
    queries = projected[:, :query_cols].reshape(
        tok_rows, kv_heads_here, query_group_count, HEAD_SIZE
    )
    key_value_rows = projected[:, query_cols:].reshape(tok_rows, kv_heads_here, 2, HEAD_SIZE)
    prev_one = shifted(key_value_rows, "seq", 1)
    prev_two = shifted(key_value_rows, "seq", 2)
    keys_all = jnp.concatenate((prev_two, prev_one, key_value_rows), axis=0)
    heads_q = query_cols // HEAD_SIZE
    window_reach_length = lax.dynamic_slice_in_dim(window, head_pos * heads_q, heads_q).reshape(
        kv_heads_here, query_group_count
    )
    key_index = jnp.arange(3 * tok_rows)
    relative = key_index[None, :] - 2 * tok_rows - offsets[:, None]
    key_pos = seq_pos * tok_rows - 2 * tok_rows + key_index
    visible = (relative[None, None] <= 0) & (
        relative[None, None] > -window_reach_length[:, :, None, None]
    )
    visible = visible & (key_pos >= 0)[None, None, None, :]
    att_scores = jnp.einsum(
        "ikgd,jkd->kgij", queries, keys_all[:, :, 0], preferred_element_type=jnp.float32
    ) * HEAD_SIZE ** (-0.5)
    masked = jnp.where(visible, att_scores, -1e30)
    row_max = jnp.max(masked, axis=-1, keepdims=True)
    probs = jnp.where(visible, jnp.exp(masked - row_max), 0.0)
    totals_row = jnp.sum(probs, axis=-1)
    probs_bf = probs.astype(jnp.bfloat16)
    context = jnp.einsum(
        "kgij,jkd->ikgd", probs_bf, keys_all[:, :, 1], preferred_element_type=jnp.float32
    )
    context = context / jnp.transpose(totals_row, (2, 0, 1))[..., None]
    attention = context.astype(jnp.bfloat16).reshape(tok_rows, query_cols)
    return (updated, attention)


def solution(mesh):
    placed = (
        P("seq", None, "head"),
        P(("seq", "head"), None),
        P(),
        P("head"),
        P("head", None),
        P(),
        P(None, "head"),
        P(None, "head", None, None),
        P(),
    )
    return jax.shard_map(
        on_device,
        mesh=mesh,
        in_specs=placed,
        out_specs=(P(("seq", "head"), None), P("seq", "head")),
        check_vma=False,
    )
```

profile of v0, /device:TPU:1, one launch (start us, length us, event | category | flops | bytes accessed | tf_op | source)
XLA Modules:
  0.0 292.2 jit_solution(12722969100295235793)
XLA Ops:
  7.3 1.5 fusion.31
  8.7 0.2 copy.71
  8.9 0.2 copy.50
  9.2 0.6 dynamic-slice
  10.4 0.2 exponential_dynamic-update-slice_fusion
  10.7 1.0 fusion.23
  11.8 34.4 %all-reduce = f32[64]{0:T(128)S(1)} all-reduce(f32[64]{0:T(128)S(1)} %get-tuple-element.135), channel_id=2, replica_groups=mesh['seq'=16,'head'=8] {'seq'}, use_global_device_ids=true, to_apply=%add | all-reduce | flops 64 | bytes 512
  46.1 0.1 reshape.235
  46.2 0.2 copy.70
  46.5 0.2 convert_maximum_fusion
  46.7 2.8 fusion.14
  49.5 21.2 %all-gather.7.cloned.1.call-done = f32[64,128,128]{2,1,0:T(8,128)} async-done(((f32[4,128,128]{2,1,0:T(8,128)}), f32[64,128,128]{2,1,0:T(8,128)}) %all-gather.7.cloned.1.call-update) | async-done | bytes 4194320 | tf_op jit(solution)/shard_map/all_gather | solution.py:14
  70.7 17.5 %while.14 = (s32[]{:T(128)}, f32[4,128,128]{2,1,0:T(8,128)S(1)}, s32[]{:T(128)}, f32[16,4]{1,0:T(8,128)S(1)}, f32[16,4,128,128]{3,2,1,0:T(8,128)}, /*index=5*/s32[]{:T(128)}, s32[]{:T(128)}) while((s32[]{:T(128)}, f32[4,128,128]{2,1,0:T(8,128)S(1)}, s32[]{:T(128)}, f32[16,4]{1,0:T(8,128)S(1)}, f32[16,4,128,128]{3,2,1,0:T(8,128)}, ...), condition=%wide.region_1.2_spmd.clone, body=%wide.region_0.1_spmd.clone.sunk | while | flops 262148 | bytes 786593 | solution.py:26
  70.7 1.0 fusion.44
  71.8 1.1 fusion.44
  72.9 1.1 fusion.44
  74.0 1.1 fusion.44
  75.1 1.1 fusion.44
  76.2 1.1 fusion.44
  77.3 1.1 fusion.44
  78.4 1.1 fusion.44
  79.5 1.1 fusion.44
  80.6 1.1 fusion.44
  81.7 1.1 fusion.44
  82.8 1.1 fusion.44
  83.9 1.1 fusion.44
  85.0 1.1 fusion.44
  86.0 1.1 fusion.44
  87.1 1.1 fusion.44
  88.2 2.3 multiply_reduce_fusion.1
  90.6 0.2 multiply_convert_fusion.2
  90.7 8.2 %convolution_convert_fusion = bf16[512,6144]{1,0:T(8,128)(2,1)} fusion(bf16[512,512]{0,1:T(8,128)(2,1)S(1)} %bitcast.93, bf16[512,6144]{1,0:T(8,128)(2,1)} %param.15), kind=kOutput, calls=%fused_computation.7 | convolution fusion | flops 3224371200 | bytes 13107200 | tf_op jit(solution)/shard_map/dot_general | solution.py:102
  99.0 70.7 %reduce-scatter.2.cloned.1.call-done = bf16[64,6144]{1,0:T(8,128)(2,1)} async-done(((bf16[512,6144]{1,0:T(8,128)(2,1)}), bf16[64,6144]{1,0:T(8,128)(2,1)}) %reduce-scatter.2.cloned.1.call-update) | async-done | bytes 786448 | tf_op jit(solution)/shard_map/reduce_scatter | solution.py:101
  169.7 1.5 multiply_reduce_fusion
  171.2 1.1 copy-done
  172.3 1.1 multiply_convert_fusion.1
  173.6 1.5 broadcast_compare_fusion
  175.0 0.3 iota_subtract_fusion
  175.3 69.4 %all-gather.5.cloned.1.call-done = bf16[512,6144]{1,0:T(8,128)(2,1)} async-done(((bf16[64,6144]{1,0:T(8,128)(2,1)}), bf16[512,6144]{1,0:T(8,128)(2,1)}) %all-gather.5.cloned.1.call-update) | async-done | bytes 6291472 | tf_op jit(solution)/shard_map/all_gather | solution.py:111
  244.7 6.2 %fusion.16 = bf16[512,256]{0,1:T(8,128)(2,1)} fusion(bf16[512,6144]{1,0:T(8,128)(2,1)} %all-gather.5.cloned.1.call-done, bf16[768,8,2,128]{3,2,1,0:T(2,128)(2,1)} %bitcast.105), kind=kOutput, calls=%fused_computation.27 | convolution fusion | flops 1610743808 | bytes 9699328 | tf_op jit(solution)/shard_map/dot_general | solution.py:113
  251.0 1.1 copy.54
  252.1 3.8 %collective-permute-start.1 = (bf16[512,1,2,128]{3,0,2,1:T(8,128)(2,1)S(1)}, bf16[512,1,2,128]{3,0,2,1:T(8,128)(2,1)S(1)}, u32[]{:S(2)}, u32[]{:S(2)}) collective-permute-start(bf16[512,1,2,128]{3,0,2,1:T(8,128)(2,1)S(1)} %copy.54), channel_id=1, source_target_pairs={{0,8},{8,16},{16,24},{24,32},{32,40},{40,48},{48,56},{56,64},{64,7... | collective-permute-start | bytes 786440 | tf_op jit(solution)/shard_map/ppermute | solution.py:32
  255.9 3.3 %collective-permute-start = (bf16[512,1,2,128]{3,0,2,1:T(8,128)(2,1)S(1)}, bf16[512,1,2,128]{3,0,2,1:T(8,128)(2,1)S(1)}, u32[]{:S(2)}, u32[]{:S(2)}) collective-permute-start(bf16[512,1,2,128]{3,0,2,1:T(8,128)(2,1)S(1)} %copy.54), channel_id=1, source_target_pairs={{0,16},{8,24},{16,32},{24,40},{32,48},{40,56},{48,64},{56,72},{64,... | collective-permute-start | bytes 786440 | tf_op jit(solution)/shard_map/ppermute | solution.py:32
  259.2 8.1 %convolution_convert_fusion.1 = bf16[512,512]{0,1:T(8,128)(2,1)S(1)} fusion(bf16[512,6144]{1,0:T(8,128)(2,1)} %all-gather.5.cloned.1.call-done, bf16[6144,512]{1,0:T(8,128)(2,1)} %param.17), kind=kOutput, calls=%fused_computation.26 | convolution fusion | flops 3221487616 | bytes 13107200 | tf_op jit(solution)/shard_map/dot_general | solution.py:112
  267.4 4.1 %fusion.1 = (f32[4,512]{1,0:T(4,128)S(1)}, f32[1536,512,4]{1,0,2:T(8,128)S(1)}) fusion(s32[512,1536]{0,1:T(8,128)S(1)} %iota_subtract_fusion, s32[4]{0:T(128)S(1)} %dynamic-slice_negate_fusion, pred[1536]{0:T(1024)(128)(4,1)S(1)} %add_compare_fusion, pred[512,1536]{0,1:T(8,128)(4,1)S(1)} %copy-done.1, bf16[512,4,128]{0,2,1:T(8,128)(2,1)S(1)} %bitcast.106, ...), kind=kOutput, calls=%fused_computation.6 | convolution fusion | flops 824178688 | bytes 17443328 | tf_op jit(solution)/shard_map/ikgd,jkd->kgij/dot_general | solution.py:135
  271.5 6.0 %fusion.2 = f32[4,512]{1,0:T(4,128)S(1)} fusion(f32[1536,512,4]{1,0,2:T(8,128)S(1)} %get-tuple-element.145, f32[4,512]{1,0:T(4,128)S(1)} %get-tuple-element.144, s32[512,1536]{0,1:T(8,128)S(1)} %iota_subtract_fusion, s32[4]{0:T(128)S(1)} %dynamic-slice_negate_fusion, pred[1536]{0:T(1024)(128)(4,1)S(1)} %add_compare_fusion, pred[512,1536]{0,1:T(8,128)(4,1)S(1)} %copy-done.1), kind=kLoop, calls=%fused_computation.8 | loop fusion | flops 25163776 | bytes 16533008 | tf_op jit(solution)/shard_map/reduce_sum | solution.py:141
  277.5 6.1 %divide_convert_fusion = bf16[512,1,4,128]{0,3,2,1:T(8,128)(2,1)} fusion(f32[1536,512,4]{1,0,2:T(8,128)S(1)} %get-tuple-element.145, f32[4,512]{1,0:T(4,128)S(1)} %get-tuple-element.144, s32[512,1536]{0,1:T(8,128)S(1)} %iota_subtract_fusion, s32[4]{0:T(128)S(1)} %dynamic-slice_negate_fusion, pred[1536]{0:T(1024)(128)(4,1)S(1)} %add_compare_fusion, ...), kind=kOutput, calls=%fused_computation.28 | convolution fusion | flops 830996480 | bytes 17451520 | tf_op jit(solution)/shard_map/kgij,jkd->ikgd/dot_general | solution.py:143
  283.6 2.0 copy.60
  (50 shorter events, 0.7 us)
Async XLA Ops:
  7.2 2.0 copy-start.7
  7.2 3.2 %copy-start.5 = (f32[32]{0:T(128)S(1)}, f32[32]{0:T(128)}, u32[]{:S(2)}) copy-start(f32[32]{0:T(128)} %param.13) | copy-start | bytes 388
  7.2 63.5 %all-gather.7.cloned.1.call-start = ((), (), s32[]{:S(2)}) async-start(), calls=%async_computation.3 | async-start | bytes 4456448 | tf_op jit(solution)/shard_map/all_gather | solution.py:14
  11.7 157.9 %reduce-scatter.2.cloned.1.call-start = ((), (), s32[]{:S(2)}) async-start(), calls=%async_computation.1 | async-start | bytes 7077888 | tf_op jit(solution)/shard_map/reduce_scatter | solution.py:101
  49.5 41.0 %copy-start.4 = (f32[512]{0:T(512)S(1)}, f32[512]{0:T(512)}, u32[]{:S(2)}) copy-start(f32[512]{0:T(512)} %param.14) | copy-start | bytes 6148
  98.9 70.8 %copy-start.2 = (bf16[64,6144]{1,0:T(8,128)(2,1)S(1)}, bf16[64,6144]{1,0:T(8,128)(2,1)}, u32[]{:S(2)}) copy-start(bf16[64,6144]{1,0:T(8,128)(2,1)} %param.12) | copy-start | bytes 2359300
  98.9 73.4 %copy-start.3 = (f32[6144]{0:T(1024)S(1)}, f32[6144]{0:T(1024)}, u32[]{:S(2)}) copy-start(f32[6144]{0:T(1024)} %param.16) | copy-start | bytes 73732
  98.9 74.5 %copy-start.6 = (s32[32]{0:T(128)S(1)}, s32[32]{0:T(128)}, u32[]{:S(2)}) copy-start(s32[32]{0:T(128)} %param.19) | copy-start | bytes 388
  98.9 145.8 %all-gather.5.cloned.1.call-start = ((), (), s32[]{:S(2)}) async-start(), calls=%async_computation.2 | async-start | bytes 7077888 | tf_op jit(solution)/shard_map/all_gather | solution.py:111
  171.2 1.2 copy-start
  252.1 15.3 %copy-start.1 = (pred[512,1536]{0,1:T(8,128)(4,1)S(1)}, pred[512,1536]{0,1:T(8,128)(4,1)}, u32[]{:S(2)}) copy-start(pred[512,1536]{0,1:T(8,128)(4,1)} %broadcast_compare_fusion) | copy-start | bytes 2359300
  252.1 15.2 %collective-permute-start.1 = (bf16[512,1,2,128]{3,0,2,1:T(8,128)(2,1)S(1)}, bf16[512,1,2,128]{3,0,2,1:T(8,128)(2,1)S(1)}, u32[]{:S(2)}, u32[]{:S(2)}) collective-permute-start(bf16[512,1,2,128]{3,0,2,1:T(8,128)(2,1)S(1)} %copy.54), channel_id=1, source_target_pairs={{0,8},{8,16},{16,24},{24,32},{32,40},{40,48},{48,56},{56,64},{64,7... | collective-permute-start | bytes 786440 | tf_op jit(solution)/shard_map/ppermute | solution.py:32
  255.9 11.4 %collective-permute-start = (bf16[512,1,2,128]{3,0,2,1:T(8,128)(2,1)S(1)}, bf16[512,1,2,128]{3,0,2,1:T(8,128)(2,1)S(1)}, u32[]{:S(2)}, u32[]{:S(2)}) collective-permute-start(bf16[512,1,2,128]{3,0,2,1:T(8,128)(2,1)S(1)} %copy.54), channel_id=1, source_target_pairs={{0,16},{8,24},{16,32},{24,40},{32,48},{40,56},{48,64},{56,72},{64,... | collective-permute-start | bytes 786440 | tf_op jit(solution)/shard_map/ppermute | solution.py:32
Sparse Core Ops, SparseCore 0:
  11.8 58.7 all-gather.6
  99.1 70.5 reduce-scatter.1
  173.6 71.0 all-gather.4
where the time goes:
time: 294 us; the launch traced here: 292 us
  waiting for transfers between devices  161 us (55%)
  matrix products  38.8 us (13%)
  blocking collectives  34.4 us (12%)
  other arithmetic  28.1 us (10%)
  between operations  14.7 us (5%)
  local copies, waits for them, and re-layouts  7.26 us (2%)
  starting transfers between devices  7.23 us (2%)
    reduce_scatter x1, waiting for transfers between devices, on_device(): lax.psum_scatter(rounded_term(jnp.dot(normed, out_weight, preferred_eleme...  70.7 us
    all_gather x1, waiting for transfers between devices, on_device(): pieces = lax.all_gather(prepared_inputs, 'head', axis=0, tiled=True)  69.4 us
    unnamed x1, blocking collectives  34.4 us
    all_gather x1, waiting for transfers between devices, carried_in(): everything = jax.tree.map(lambda part: lax.all_gather(part, axis), value)  21.2 us
    select_n x16, other arithmetic, hop(): return jax.tree.map(lambda a, b: jnp.where(reached, a, b), new, before)  16.9 us
    dot_general x1, matrix products, on_device(): jnp.dot(normed, out_weight, preferred_element_type=jnp.float32)  8.16 us
    dot_general x1, matrix products, on_device(): jnp.dot(pieces, query_weight, preferred_element_type=jnp.float32)  8.05 us
    ppermute x2, starting transfers between devices, shifted(): lax.ppermute(value, axis, [(source, source + steps) for source in range(l...  7.11 us
  transfers between devices with their start and end apart: 5, of which 3 were waited for; matrix products, arithmetic and copies ran while one was open for 5% of the time, Pallas kernels for 0%

commit v1 on v0

v1 whole, which is shorter than its diff:
```python
import functools

import jax
import jax.numpy as jnp
from jax import lax
from jax.experimental import pallas as pl
from jax.experimental.pallas import tpu as pltpu
from jax.sharding import PartitionSpec as P

MESH = pl.DeviceIdType.MESH
F32 = jnp.float32
BF16 = jnp.bfloat16
HEAD = 128
EPS = 1e-06
TOK = 512
MODEL = 6144
NCH = 4
CH = MODEL // NCH
HALF = CH // 2
NP = 2
R = 64 // NP
QKV = 768


def coords():
    s, h = lax.axis_index("seq"), lax.axis_index("head")
    return lax.div(s, 8), lax.rem(lax.div(s, 2), 4), lax.rem(s, 2), lax.div(h, 4), lax.rem(h, 4)


def place(x, y, c, z):
    x, y, z = lax.rem(x + 4, 4), lax.rem(y + 4, 4), lax.rem(z + 4, 4)
    return (lax.div(x, 2) * 8 + y * 2 + c, lax.rem(x, 2) * 4 + z)


def dot(a, b):
    return jnp.dot(a, b, preferred_element_type=F32)


def dot_t(a, b):
    return lax.dot_general(a, b, (((1,), (1,)), ((), ())), preferred_element_type=F32)


def rows_of(shape):
    return lax.broadcasted_iota(jnp.int32, shape, 0)


def cols_of(shape):
    return lax.broadcasted_iota(jnp.int32, shape, 1)


def body(
    qkv,
    residual,
    decay,
    lgain,
    wo_hbm,
    again,
    wq_hbm,
    wkv_hbm,
    window,
    upd_out,
    att_out,
    wo_own,
    wo_par,
    wq_own,
    wq_par,
    s_own,
    s_pair,
    t_send,
    t_recv,
    p_all,
    intra,
    normed,
    nrecv,
    part,
    a_p,
    a_m,
    b_p,
    b_m,
    upd,
    gath,
    acc,
    qbuf,
    kvbuf,
    stq,
    stkv,
    own_sem,
    w_s,
    w_r,
    sp_s,
    sp_r,
    t_s,
    t_r,
    n_s,
    n_r,
    a_s,
    a_r,
    b_s,
    b_r,
    g_s,
    g_r,
    x_s,
    x_r,
    h_s,
    h_r,
):
    xh, y, c, xl, z = coords()
    x = 2 * xh + xl
    s, h = lax.axis_index("seq"), lax.axis_index("head")
    other = lax.rem(h + 4, 8)
    m = xh * 4 + y
    e = lax.rem(y, 2)
    z_up, z_dn = lax.rem(z + 1, 4), lax.rem(z + 3, 4)
    z_far = lax.rem(z + 2, 4)
    to_zu, to_zd = place(x, y, c, z + 1), place(x, y, c, z - 1)
    to_xu, to_xd = place(x + 1, y, c, z), place(x - 1, y, c, z)
    to_yu, to_yd = place(x, y + 1, c, z), place(x, y - 1, c, z)
    to_core = (s + 1 - 2 * c, h)
    to_pair = (s, other)
    sent = []

    def send(src, dst, ssem, rsem, target, later=True):
        cp = pltpu.make_async_remote_copy(
            src_ref=src, dst_ref=dst, send_sem=ssem, recv_sem=rsem,
            device_id=target, device_id_type=MESH,
        )
        cp.start()
        if later:
            sent.append(cp)
        return cp

    def arrived(dst, sem):
        pltpu.make_async_copy(dst, dst, sem).wait()

    bar = pltpu.get_barrier_semaphore()
    peers = [to_zu, to_zd, to_xu, to_xd, to_core]
    for k in range(1, 8):
        mm = lax.rem(m + k, 8)
        peers.append((mm * 2 + c, h))
    for step in (1, 2, 14, 15):
        there = lax.rem(s + step, 16)
        peers += [(there, h), (there, other)]
    for p in peers:
        pl.semaphore_signal(bar, 1, device_id=p, device_id_type=MESH)
    pl.semaphore_wait(bar, len(peers))

    own = [
        pltpu.make_async_copy(wo_hbm, wo_own, own_sem.at[0]),
        pltpu.make_async_copy(wq_hbm, wq_own.at[:, pl.ds(0, 512)], own_sem.at[1]),
        pltpu.make_async_copy(wkv_hbm, wq_own.at[:, pl.ds(512, 256)], own_sem.at[2]),
    ]

    hbm_of = (wo_hbm, wq_hbm, wkv_hbm)

    def region(a, k, cc, first, count, hbm=False):
        if a == 0:
            rows = pl.ds(pl.multiple_of(cc * 256 + first * 64, 64), count * 64)
            ref = wo_hbm if hbm else wo_par
            return ref.at[rows, pl.ds(k * CH, CH)]
        rows = pl.ds(pl.multiple_of(cc * 3072 + k * 768 + first * 192, 64), count * 192)
        if hbm:
            return hbm_of[a].at[rows]
        return wq_par.at[rows, pl.ds(0, 512) if a == 1 else pl.ds(512, 256)]

    def push(a, k):
        for d, target in ((0, to_xu), (1, to_xd)):
            send(
                region(a, k, c, e * 2 + d, 1, True), region(a, k, c, e * 2 + d, 1),
                w_s.at[a, k, d], w_r.at[a, k, d], target,
            )

    def relay(a, k):
        for d, target in ((0, to_yu), (1, to_yd)):
            piece = region(a, k, c, e * 2 + d, 1)
            arrived(piece, w_r.at[a, k, d])
            send(piece, piece, w_s.at[a, k, 2 + d], w_r.at[a, k, 2 + d], target)

    def mirror(a, k):
        for d in (0, 1):
            arrived(region(a, k, c, (1 - e) * 2 + d, 1), w_r.at[a, k, 2 + d])
        piece = region(a, k, c, 0, 4)
        send(piece, piece, w_s.at[a, k, 4], w_r.at[a, k, 4], to_core)

    def ready(a, k):
        arrived(region(a, k, 1 - c, 0, 4), w_r.at[a, k, 4])

    push(0, 0)
    for cp in own:
        cp.start()

    rate = [decay[h * 4 + i] for i in range(4)]

    def head_of(i):
        return pl.ds(i * HEAD, HEAD)

    for i in range(4):
        back = (TOK - 1 - rows_of((TOK, HEAD))).astype(F32)
        keys = qkv[1, :, head_of(i)].astype(F32) * jnp.exp(-rate[i] * back)
        s_own[i] = lax.dot_general(
            keys.astype(BF16), qkv[2, :, head_of(i)], (((0,), (0,)), ((), ())),
            preferred_element_type=F32,
        )
    send(s_own, s_pair, sp_s.at[0], sp_r.at[0], to_core)

    def within(i):
        for t in range(4):
            n = HEAD * (t + 1)
            lq = qkv[0, pl.ds(t * HEAD, HEAD), head_of(i)]
            sc = dot_t(lq, qkv[1, pl.ds(0, n), head_of(i)])
            gap = (rows_of((HEAD, n)) + t * HEAD - cols_of((HEAD, n))).astype(F32)
            fade = jnp.where(gap >= 0, jnp.exp(-rate[i] * jnp.maximum(gap, 0.0)), 0.0)
            intra[pl.ds(t * HEAD, HEAD), head_of(i)] = dot(
                (sc * fade).astype(BF16), qkv[2, pl.ds(0, n), head_of(i)]
            )

    within(0)
    arrived(s_pair, sp_r.at[0])
    for i in range(2):
        hd = 2 * c + i
        dd = decay[h * 4 + hd]
        mine, theirs = s_own[hd], s_pair[hd]
        fade = jnp.exp(jnp.full((HEAD, HEAD), -dd * TOK, F32))
        first, second = jnp.where(c == 0, mine, theirs), jnp.where(c == 0, theirs, mine)
        t_send[i] = (fade * first + second).astype(BF16)
    for mm in range(1, 8):

        @pl.when(m < mm)
        def _(mm=mm):
            send(t_send, t_recv.at[m], t_s.at[mm - 1], t_r.at[m], (mm * 2 + c, h), False)

    push(0, 1)
    push(0, 2)
    within(1)
    within(2)
    within(3)
    relay(0, 0)
    for i in range(2):
        p_all[2 * c + i] = jnp.zeros((HEAD, HEAD), F32)
    for mm in range(7):

        @pl.when(mm < m)
        def _(mm=mm):
            arrived(t_recv.at[mm], t_r.at[mm])
            for i in range(2):
                dd = decay[h * 4 + 2 * c + i]
                gone = (m - 1 - mm).astype(F32) * (2.0 * TOK)
                p_all[2 * c + i] += (
                    jnp.exp(jnp.full((HEAD, HEAD), -dd * gone, F32)) * t_recv[mm, i].astype(F32)
                )

    half_p = p_all.at[pl.ds(2 * c, 2)]
    send(half_p, half_p, sp_s.at[1], sp_r.at[1], to_core)
    relay(0, 1)
    mirror(0, 0)
    arrived(p_all.at[pl.ds(2 * (1 - c), 2)], sp_r.at[1])

    def finish(lo):
        for i in range(4):
            span = pl.ds(pl.multiple_of(lo, 256), 256)
            before = p_all[i]
            fade = jnp.exp(jnp.full((HEAD, HEAD), -rate[i] * TOK, F32))
            start = jnp.where(c == 0, before, fade * before + s_pair[i])
            ahead = (rows_of((256, HEAD)) + (lo + 1)).astype(F32)
            lq = qkv[0, span, head_of(i)].astype(F32) * jnp.exp(-rate[i] * ahead)
            full = intra[span, head_of(i)] + jnp.dot(
                lq, start, preferred_element_type=F32, precision=lax.Precision.HIGHEST
            )
            scale = lax.rsqrt(jnp.mean(full * full, axis=-1, keepdims=True) + EPS)
            normed[span, head_of(i)] = (full * scale * lgain[:, head_of(i)]).astype(BF16)

    finish((1 - xl) * 256)
    give = normed.at[pl.ds(pl.multiple_of((1 - xl) * 256, 256), 256)]
    send(give, nrecv, n_s.at[0], n_r.at[0], to_pair)
    push(0, 3)
    for k in range(4):
        push(1, k)
        push(2, k)
    finish(xl * 256)
    relay(0, 2)
    mirror(0, 1)
    own[0].wait()
    arrived(nrecv, n_r.at[0])

    def block(zz):
        return pl.ds(pl.multiple_of(zz * 64, 64), 64)

    keep = pl.ds(pl.multiple_of(xl * 256, 256), 256)

    def project(k):
        ready(0, k)

        def tile(j, carry):
            at = pl.ds(pl.multiple_of(k * CH + j * 512, 512), 512)
            total = dot(normed[keep, :], wo_own[:, at]) + dot(nrecv[...], wo_par[:, at])
            part[:, at] = total.astype(BF16)
            return carry

        lax.fori_loop(0, CH // 512, tile, 0)
        left, right = pl.ds(k * CH, HALF), pl.ds(k * CH + HALF, HALF)
        slot = pl.ds(k * HALF, HALF)
        send(part.at[block(z_far), left], a_p.at[:, slot], a_s.at[k, 0], a_r.at[k, 0], to_zu)
        send(part.at[block(z_far), right], a_m.at[:, slot], a_s.at[k, 1], a_r.at[k, 1], to_zd)

    def join(k):
        left, right = pl.ds(k * CH, HALF), pl.ds(k * CH + HALF, HALF)
        slot, chunk = pl.ds(k * HALF, HALF), pl.ds(k * CH, CH)
        arrived(a_p.at[:, slot], a_r.at[k, 0])
        part[block(z_up), left] = (
            part[block(z_up), left].astype(F32) + a_p[:, slot].astype(F32)
        ).astype(BF16)
        send(part.at[block(z_up), chunk], b_p.at[:, chunk], b_s.at[k, 0], b_r.at[k, 0], to_zu)
        arrived(a_m.at[:, slot], a_r.at[k, 1])
        part[block(z_dn), right] = (
            part[block(z_dn), right].astype(F32) + a_m[:, slot].astype(F32)
        ).astype(BF16)
        send(part.at[block(z_dn), chunk], b_m.at[:, chunk], b_s.at[k, 1], b_r.at[k, 1], to_zd)

    def close(k):
        chunk = pl.ds(k * CH, CH)
        arrived(b_p.at[:, chunk], b_r.at[k, 0])
        arrived(b_m.at[:, chunk], b_r.at[k, 1])
        total = (
            residual[:, chunk].astype(F32) + part[block(z), chunk].astype(F32)
            + b_p[:, chunk].astype(F32) + b_m[:, chunk].astype(F32)
        )
        upd[:, chunk] = total
        return jnp.sum(total * total, axis=-1, keepdims=True)

    project(0)
    mirror(0, 2)
    project(1)
    join(0)
    relay(0, 3)
    project(2)
    join(1)
    mirror(0, 3)
    project(3)
    join(2)
    join(3)
    relay(1, 0)
    relay(2, 0)
    square = close(0)
    square += close(1)
    relay(1, 1)
    relay(2, 1)
    mirror(1, 0)
    mirror(2, 0)
    square += close(2)
    square += close(3)
    scale = lax.rsqrt(square * (1.0 / MODEL) + EPS)
    store = pltpu.make_async_copy(upd, upd_out, own_sem.at[3])
    store.start()

    for p in range(NP):
        row = pl.ds(p * R, R)
        gath[p, z] = (upd[row, :] * scale[p * R : (p + 1) * R] * again[...]).astype(BF16)
        mine = gath.at[p, z]
        send(mine, mine, g_s.at[p, 0], g_r.at[p, 0], to_zu)
        send(mine, mine, g_s.at[p, 1], g_r.at[p, 1], to_zd)

    def forward(p):
        below, above = gath.at[p, z_dn], gath.at[p, z_up]
        left, right = pl.ds(0, MODEL // 2), pl.ds(MODEL // 2, MODEL // 2)
        arrived(below, g_r.at[p, 0])
        send(below.at[:, left], below.at[:, left], g_s.at[p, 2], g_r.at[p, 2], to_zu)
        arrived(above, g_r.at[p, 1])
        send(above.at[:, right], above.at[:, right], g_s.at[p, 3], g_r.at[p, 3], to_zd)

    def gathered(p):
        far = gath.at[p, z_far]
        arrived(far.at[:, pl.ds(0, MODEL // 2)], g_r.at[p, 2])
        arrived(far.at[:, pl.ds(MODEL // 2, MODEL // 2)], g_r.at[p, 3])

    mine_half, mine_kv = pl.ds(xl * 4, 4), pl.ds(16 + xl * 4, 4)

    def second(p):
        acc[...] = jnp.zeros_like(acc)

        def deep(j, carry):
            at = pl.ds(pl.multiple_of(j * 1024, 1024), 1024)
            lhs = gath[p, :, :, at].reshape(4 * R, 1024)
            acc[:, pl.ds(0, QKV)] += dot(lhs, wq_own[at, :])
            acc[:, pl.ds(QKV, QKV)] += dot(lhs, wq_par[at, :])
            return carry

        lax.fori_loop(0, 6, deep, 0)
        stkv[p] = acc[:, pl.ds(QKV + 512, 256)].astype(BF16).reshape(4, R, 256)
        kvbuf[mine_kv, p] = acc[:, pl.ds(512, 256)].astype(BF16).reshape(4, R, 256)
        send(stkv.at[p], kvbuf.at[mine_kv, p], x_s.at[p, 0], x_r.at[p, 0], to_pair)
        for step in (1, 2):

            @pl.when(s + step < 16)
            def _(step=step):
                slot = kvbuf.at[pl.ds(16 - 8 * step + xl * 4, 4), p]
                sem = h_r.at[p, step - 1, xl]
                send(kvbuf.at[mine_kv, p], slot, h_s.at[p, step - 1, 0], sem, (s + step, h), False)
                send(stkv.at[p], slot, h_s.at[p, step - 1, 1], sem, (s + step, other), False)

        stq[p] = acc[:, pl.ds(QKV, 512)].astype(BF16).reshape(4, R, 512)
        send(stq.at[p], qbuf.at[mine_half, p], x_s.at[p, 1], x_r.at[p, 1], to_pair)
        qbuf[mine_half, p] = acc[:, pl.ds(0, 512)].astype(BF16).reshape(4, R, 512)

    relay(1, 2)
    relay(2, 2)
    mirror(1, 1)
    mirror(2, 1)
    forward(0)
    relay(1, 3)
    relay(2, 3)
    mirror(1, 2)
    mirror(2, 2)
    forward(1)
    mirror(1, 3)
    mirror(2, 3)
    own[1].wait()
    own[2].wait()
    for k in range(4):
        ready(1, k)
        ready(2, k)
    gathered(0)
    second(0)
    gathered(1)
    second(1)

    @pl.when(s < 1)
    def _():
        kvbuf[pl.ds(8, 8)] = jnp.zeros((8, NP, R, 256), BF16)

    @pl.when(s < 2)
    def _():
        kvbuf[pl.ds(0, 8)] = jnp.zeros((8, NP, R, 256), BF16)

    for p in range(NP):
        arrived(kvbuf.at[pl.ds(16 + (1 - xl) * 4, 4), p], x_r.at[p, 0])
        for step in (1, 2):

            @pl.when(s - step >= 0)
            def _(p=p, step=step):
                for hf in (0, 1):
                    slot = kvbuf.at[pl.ds(16 - 8 * step + hf * 4, 4), p]
                    arrived(slot, h_r.at[p, step - 1, hf])

        arrived(qbuf.at[pl.ds((1 - xl) * 4, 4), p], x_r.at[p, 1])

    def attend(t, carry):
        shape = (HEAD, 1152)
        row, col = rows_of(shape), cols_of(shape)
        gap = col - row
        early = 1024 - s * TOK - t * HEAD
        keys = kvbuf[pl.ds(2 * t, 18), :, :, pl.ds(0, HEAD)].reshape(1152, HEAD)
        vals = kvbuf[pl.ds(2 * t, 18), :, :, pl.ds(HEAD, HEAD)].reshape(1152, HEAD)
        for i in range(4):
            reach = window[h * 4 + i]
            seen = (gap <= 1024) & (gap > 1024 - reach) & (col >= early)
            q = qbuf[pl.ds(2 * t, 2), :, :, head_of(i)].reshape(HEAD, HEAD)
            sc = dot_t(q, keys) * (HEAD**-0.5)
            sc = jnp.where(seen, sc, -1e30)
            top = jnp.max(sc, axis=-1, keepdims=True)
            pr = jnp.where(seen, jnp.exp(sc - top), 0.0)
            total = jnp.sum(pr, axis=-1, keepdims=True)
            out = dot(pr.astype(BF16), vals) / total
            att_out[pl.ds(pl.multiple_of(t * HEAD, HEAD), HEAD), head_of(i)] = out.astype(BF16)
        return carry

    lax.fori_loop(0, 4, attend, 0)

    store.wait()
    for cp in sent:
        cp.wait_send()
    for mm in range(1, 8):

        @pl.when(m < mm)
        def _(mm=mm):
            pltpu.make_async_copy(t_send, t_send, t_s.at[mm - 1]).wait()

    for p in range(NP):
        for step in (1, 2):

            @pl.when(s + step < 16)
            def _(p=p, step=step):
                pltpu.make_async_copy(stkv.at[p], stkv.at[p], h_s.at[p, step - 1, 0]).wait()
                pltpu.make_async_copy(stkv.at[p], stkv.at[p], h_s.at[p, step - 1, 1]).wait()


def on_device(
    lightning_qkv,
    residual,
    decay_rate,
    lightning_gain,
    out_weight,
    attn_gain,
    query_weight,
    key_value_weight,
    window,
):
    vmem = pl.BlockSpec(memory_space=pltpu.VMEM)
    smem = pl.BlockSpec(memory_space=pltpu.SMEM)
    anyw = pl.BlockSpec(memory_space=pl.ANY)
    dma = pltpu.SemaphoreType.DMA
    V = pltpu.VMEM
    return pl.pallas_call(
        body,
        out_shape=(
            jax.ShapeDtypeStruct((64, MODEL), F32),
            jax.ShapeDtypeStruct((TOK, 512), BF16),
        ),
        in_specs=[vmem, vmem, smem, vmem, anyw, vmem, anyw, anyw, smem],
        out_specs=(anyw, vmem),
        scratch_shapes=[
            V((512, MODEL), BF16),
            V((512, MODEL), BF16),
            V((MODEL, QKV), BF16),
            V((MODEL, QKV), BF16),
            V((4, HEAD, HEAD), F32),
            V((4, HEAD, HEAD), F32),
            V((2, HEAD, HEAD), BF16),
            V((7, 2, HEAD, HEAD), BF16),
            V((4, HEAD, HEAD), F32),
            V((TOK, 512), F32),
            V((TOK, 512), BF16),
            V((256, 512), BF16),
            V((256, MODEL), BF16),
            V((64, MODEL // 2), BF16),
            V((64, MODEL // 2), BF16),
            V((64, MODEL), BF16),
            V((64, MODEL), BF16),
            V((64, MODEL), F32),
            V((NP, 4, R, MODEL), BF16),
            V((4 * R, 2 * QKV), F32),
            V((8, NP, R, 512), BF16),
            V((24, NP, R, 256), BF16),
            V((NP, 4, R, 512), BF16),
            V((NP, 4, R, 256), BF16),
            dma((4,)),
            dma((3, 4, 5)),
            dma((3, 4, 5)),
            dma((2,)),
            dma((2,)),
            dma((7,)),
            dma((7,)),
            dma((1,)),
            dma((1,)),
            dma((NCH, 2)),
            dma((NCH, 2)),
            dma((NCH, 2)),
            dma((NCH, 2)),
            dma((NP, 4)),
            dma((NP, 4)),
            dma((NP, 2)),
            dma((NP, 2)),
            dma((NP, 2, 2)),
            dma((NP, 2, 2)),
        ],
        compiler_params=pltpu.CompilerParams(
            collective_id=0, has_side_effects=True, vmem_limit_bytes=60 * 2**20
        ),
    )(
        jnp.transpose(lightning_qkv, (1, 0, 2)),
        residual,
        decay_rate,
        lightning_gain.reshape(1, 512),
        out_weight,
        attn_gain.reshape(1, MODEL),
        query_weight,
        key_value_weight.reshape(MODEL, 256),
        window,
    )


def solution(mesh):
    placed = (
        P("seq", None, "head"),
        P(("seq", "head"), None),
        P(),
        P("head"),
        P("head", None),
        P(),
        P(None, "head"),
        P(None, "head", None, None),
        P(),
    )
    return jax.shard_map(
        on_device,
        mesh=mesh,
        in_specs=placed,
        out_specs=(P(("seq", "head"), None), P("seq", "head")),
        check_vma=False,
    )
```

time: 294 us -> 128 us (0.44)
  waiting for transfers between devices: 161 us -> 0 us
  Pallas kernels: 0 us -> 120 us
  matrix products: 38.8 us -> 0 us
  blocking collectives: 34.4 us -> 0 us
  other arithmetic: 28.1 us -> 0 us
  between operations: 14.7 us -> 0.65 us
  starting transfers between devices: 7.23 us -> 0 us
    pallas_call x0 -> x1, Pallas kernels: none -> 120 us  [on_device(): pl.pallas_call(body, out_shape=(jax.ShapeDtypeStruct((64, MODEL), F32), j...]
    all_gather x2 -> x0, waiting for transfers between devices: 90.6 us -> none  [the longest x1 69.4 us: on_device(): pieces = lax.all_gather(prepared_inputs, 'head', axis=0, tiled=True)]
    reduce_scatter x1 -> x0, waiting for transfers between devices: 70.7 us -> none  [on_device(): lax.psum_scatter(rounded_term(jnp.dot(normed, out_weight, preferred_eleme...]
    dot_general x8 -> x0, matrix products: 38.8 us -> none  [the longest x1 8.16 us: on_device(): jnp.dot(normed, out_weight, preferred_element_type=jnp.float32)]
    unnamed x1 -> x0, blocking collectives: 34.4 us -> none
    select_n x16 -> x0, other arithmetic: 16.9 us -> none  [hop(): return jax.tree.map(lambda a, b: jnp.where(reached, a, b), new, before)]
    reduce_sum x2 -> x0, other arithmetic: 7.53 us -> none  [the longest x1 6.04 us: on_device(): totals_row = jnp.sum(probs, axis=-1)]
    ppermute x2 -> x0, starting transfers between devices: 7.11 us -> none  [shifted(): lax.ppermute(value, axis, [(source, source + steps) for source in range(l...]
  transfers between devices with their start and end apart: 5 -> 0, of which waited for: 3 -> 0; matrix products, arithmetic and copies ran while one was open for 5% -> 0% of each run, Pallas kernels for 0% -> 0%
where the time goes in v1:
time: 128 us
  Pallas kernels  120 us (94%)
  local copies, waits for them, and re-layouts  7.47 us (6%)
    pallas_call x1, Pallas kernels, on_device(): pl.pallas_call(body, out_shape=(jax.ShapeDtypeStruct((64, MODEL), F32), j...  120 us
    unnamed x5, local copies, waits for them, and re-layouts  7.47 us

profile of v1, /device:TPU:1, one launch (start us, length us, event | category | flops | bytes accessed | tf_op | source)
XLA Modules:
  0.0 127.9 jit_solution(2898680175635546189)
XLA Ops:
  0.6 4.0 %copy.13 = bf16[768,8,2,128]{3,1,2,0:T(8,128)(2,1)} copy(bf16[768,8,2,128]{3,2,1,0:T(2,128)(2,1)} %bitcast.9) | data formatting | bytes 6291456
  4.6 119.8 %shard_map.104 = (f32[64,6144]{1,0:T(8,128)}, bf16[512,512]{1,0:T(8,128)(2,1)}) custom-call(bf16[3,512,512]{2,1,0:T(8,128)(2,1)} %bitcast.10, bf16[64,6144]{1,0:T(8,128)(2,1)} %residual.1, f32[32]{0:T(128)} %decay.1, f32[1,512]{1,0:T(1,128)} %bitcast.12, bf16[512,6144]{1,0:T(8,128)(2,1)} %wo_hbm.1, f32[1,6144]{1,0:T(1,128)} %bitcast.11, ...), custom_call_target="tpu_custom_call" | custom-call | tf_op jit(solution)/shard_map/pallas_call | solution.py:501
  124.4 0.0 copy-start
  124.4 2.7 %copy.16 = f32[64,6144]{1,0:T(8,128)} copy(f32[64,6144]{1,0:T(8,128)} %get-tuple-element.4) | data formatting | bytes 3145728
  127.1 0.0 copy-done
  127.1 0.8 copy.17
Async XLA Ops:
  124.4 2.7 %copy-start = (bf16[512,512]{1,0:T(8,128)(2,1)S(1)}, bf16[512,512]{1,0:T(8,128)(2,1)}, u32[]{:S(2)}) copy-start(bf16[512,512]{1,0:T(8,128)(2,1)} %get-tuple-element.5) | copy-start | bytes 1572868

commit v2 on v1

--- a/solution.py
+++ b/solution.py
@@ -14,7 +14,7 @@
 EPS = 1e-06
 TOK = 512
 MODEL = 6144
-NCH = 4
+NCH = 8
 CH = MODEL // NCH
 HALF = CH // 2
 NP = 2
@@ -64,13 +64,17 @@
     wo_par,
     wq_own,
     wq_par,
+    wkv_own,
+    wkv_par,
+    wide,
     s_own,
     s_pair,
     t_send,
     t_recv,
     p_all,
     intra,
-    normed,
+    nsend,
+    nown,
     nrecv,
     part,
     a_p,
@@ -113,7 +117,7 @@
     z_up, z_dn = lax.rem(z + 1, 4), lax.rem(z + 3, 4)
     z_far = lax.rem(z + 2, 4)
     to_zu, to_zd = place(x, y, c, z + 1), place(x, y, c, z - 1)
-    to_xu, to_xd = place(x + 1, y, c, z), place(x - 1, y, c, z)
+    to_outer = place(x + 2 * xl - 1, y, c, z)
     to_yu, to_yd = place(x, y + 1, c, z), place(x, y - 1, c, z)
     to_core = (s + 1 - 2 * c, h)
     to_pair = (s, other)
@@ -133,7 +137,7 @@
         pltpu.make_async_copy(dst, dst, sem).wait()
 
     bar = pltpu.get_barrier_semaphore()
-    peers = [to_zu, to_zd, to_xu, to_xd, to_core]
+    peers = [to_zu, to_zd, to_pair, to_outer, to_core]
     for k in range(1, 8):
         mm = lax.rem(m + k, 8)
         peers.append((mm * 2 + c, h))
@@ -142,49 +146,60 @@
         peers += [(there, h), (there, other)]
     for p in peers:
         pl.semaphore_signal(bar, 1, device_id=p, device_id_type=MESH)
-    pl.semaphore_wait(bar, len(peers))
 
     own = [
         pltpu.make_async_copy(wo_hbm, wo_own, own_sem.at[0]),
         pltpu.make_async_copy(wq_hbm, wq_own.at[:, pl.ds(0, 512)], own_sem.at[1]),
-        pltpu.make_async_copy(wkv_hbm, wq_own.at[:, pl.ds(512, 256)], own_sem.at[2]),
+        pltpu.make_async_copy(wkv_hbm, wkv_own, own_sem.at[2]),
     ]
 
     hbm_of = (wo_hbm, wq_hbm, wkv_hbm)
 
-    def region(a, k, cc, first, count, hbm=False):
+    def region(a, k, cc, par, d, hbm=False):
+        whole, cut = (128, 48) if a == 0 else (384 * a, 176 * a)
+        base = cc * 256 if a == 0 else cc * 8 * whole + k * 2 * whole
+        count = (cut, whole - cut, 2 * whole)[d]
+        base = base + par * whole + (cut if d == 1 else 0)
+        rows = pl.ds(pl.multiple_of(base, 16), count)
         if a == 0:
-            rows = pl.ds(pl.multiple_of(cc * 256 + first * 64, 64), count * 64)
-            ref = wo_hbm if hbm else wo_par
-            return ref.at[rows, pl.ds(k * CH, CH)]
-        rows = pl.ds(pl.multiple_of(cc * 3072 + k * 768 + first * 192, 64), count * 192)
+            return (wo_hbm if hbm else wo_par).at[rows, pl.ds(k * CH, CH)]
         if hbm:
             return hbm_of[a].at[rows]
-        return wq_par.at[rows, pl.ds(0, 512) if a == 1 else pl.ds(512, 256)]
-
-    def push(a, k):
-        for d, target in ((0, to_xu), (1, to_xd)):
-            send(
-                region(a, k, c, e * 2 + d, 1, True), region(a, k, c, e * 2 + d, 1),
-                w_s.at[a, k, d], w_r.at[a, k, d], target,
-            )
+        return wq_par.at[rows, pl.ds(0, 512)] if a == 1 else wkv_par.at[rows]
+
+    def push(a, k, d):
+        send(
+            region(a, k, c, e, d, True), region(a, k, c, e, d),
+            w_s.at[a, k, d], w_r.at[a, k, d], (to_pair, to_outer)[d],
+        )
 
     def relay(a, k):
-        for d, target in ((0, to_yu), (1, to_yd)):
-            piece = region(a, k, c, e * 2 + d, 1)
+        for d in (0, 1):
+            piece = region(a, k, c, e, d)
             arrived(piece, w_r.at[a, k, d])
+            target = (to_yu, to_yd)[(d + k) % 2]
             send(piece, piece, w_s.at[a, k, 2 + d], w_r.at[a, k, 2 + d], target)
 
     def mirror(a, k):
         for d in (0, 1):
-            arrived(region(a, k, c, (1 - e) * 2 + d, 1), w_r.at[a, k, 2 + d])
-        piece = region(a, k, c, 0, 4)
+            arrived(region(a, k, c, 1 - e, d), w_r.at[a, k, 2 + d])
+        piece = region(a, k, c, 0, 2)
         send(piece, piece, w_s.at[a, k, 4], w_r.at[a, k, 4], to_core)
 
     def ready(a, k):
-        arrived(region(a, k, 1 - c, 0, 4), w_r.at[a, k, 4])
-
-    push(0, 0)
+        arrived(region(a, k, 1 - c, 0, 2), w_r.at[a, k, 4])
+
+    def separate(raw, to, first, count):
+        def piece(j, carry):
+            at = pl.multiple_of(first + j * 384, 64)
+            wide[...] = raw[pl.ds(pl.multiple_of(2 * at, 128), 768), :].astype(F32)
+            for i in (0, 1):
+                cols = pl.ds(512 + i * HEAD, HEAD)
+                to[pl.ds(at, 384), cols] = wide[pl.ds(i, 384, stride=2), :].astype(BF16)
+            return carry
+
+        lax.fori_loop(0, count // 384, piece, 0)
+
     for cp in own:
         cp.start()
 
@@ -200,6 +215,9 @@
             keys.astype(BF16), qkv[2, :, head_of(i)], (((0,), (0,)), ((), ())),
             preferred_element_type=F32,
         )
+    pl.semaphore_wait(bar, len(peers))
+    push(0, 0, 1)
+    push(0, 0, 0)
     send(s_own, s_pair, sp_s.at[0], sp_r.at[0], to_core)
 
     def within(i):
@@ -228,12 +246,18 @@
         def _(mm=mm):
             send(t_send, t_recv.at[m], t_s.at[mm - 1], t_r.at[m], (mm * 2 + c, h), False)
 
-    push(0, 1)
-    push(0, 2)
+    for k in range(1, NCH):
+        push(0, k, 1)
+    for k in range(1, 6):
+        push(0, k, 0)
+    for k in range(4):
+        push(1, k, 1)
+        push(2, k, 1)
     within(1)
     within(2)
     within(3)
     relay(0, 0)
+    relay(0, 1)
     for i in range(2):
         p_all[2 * c + i] = jnp.zeros((HEAD, HEAD), F32)
     for mm in range(7):
@@ -249,104 +273,134 @@
                 )
 
     half_p = p_all.at[pl.ds(2 * c, 2)]
-    send(half_p, half_p, sp_s.at[1], sp_r.at[1], to_core)
-    relay(0, 1)
-    mirror(0, 0)
+    across = send(half_p, half_p, sp_s.at[1], sp_r.at[1], to_core, False)
+    relay(0, 2)
     arrived(p_all.at[pl.ds(2 * (1 - c), 2)], sp_r.at[1])
 
-    def finish(lo):
+    order = (z_far, z_up, z_dn, z)
+
+    def finish(to, lo, j):
+        first = lo + order[j] * 64
+        span, out = pl.ds(pl.multiple_of(first, 64), 64), pl.ds(j * 64, 64)
         for i in range(4):
-            span = pl.ds(pl.multiple_of(lo, 256), 256)
-            before = p_all[i]
-            fade = jnp.exp(jnp.full((HEAD, HEAD), -rate[i] * TOK, F32))
-            start = jnp.where(c == 0, before, fade * before + s_pair[i])
-            ahead = (rows_of((256, HEAD)) + (lo + 1)).astype(F32)
+            ahead = (rows_of((64, HEAD)) + (first + 1)).astype(F32)
             lq = qkv[0, span, head_of(i)].astype(F32) * jnp.exp(-rate[i] * ahead)
             full = intra[span, head_of(i)] + jnp.dot(
-                lq, start, preferred_element_type=F32, precision=lax.Precision.HIGHEST
+                lq, p_all[i], preferred_element_type=F32, precision=lax.Precision.HIGHEST
             )
             scale = lax.rsqrt(jnp.mean(full * full, axis=-1, keepdims=True) + EPS)
-            normed[span, head_of(i)] = (full * scale * lgain[:, head_of(i)]).astype(BF16)
-
-    finish((1 - xl) * 256)
-    give = normed.at[pl.ds(pl.multiple_of((1 - xl) * 256, 256), 256)]
-    send(give, nrecv, n_s.at[0], n_r.at[0], to_pair)
-    push(0, 3)
+            to[out, head_of(i)] = (full * scale * lgain[:, head_of(i)]).astype(BF16)
+
+    def four(j):
+        return pl.ds(j * 64, 64)
+
+    across.wait_send()
+
+    @pl.when(c == 1)
+    def _():
+        for i in range(4):
+            fade = jnp.exp(jnp.full((HEAD, HEAD), -rate[i] * TOK, F32))
+            p_all[i] = fade * p_all[i] + s_pair[i]
+
+    for j in range(4):
+        finish(nsend, (1 - xl) * 256, j)
+        send(nsend.at[four(j)], nrecv.at[four(j)], n_s.at[j], n_r.at[j], to_pair)
+    push(0, 6, 0)
+    push(0, 7, 0)
     for k in range(4):
-        push(1, k)
-        push(2, k)
-    finish(xl * 256)
-    relay(0, 2)
+        push(1, k, 0)
+        push(2, k, 0)
+    relay(0, 3)
+    mirror(0, 0)
+    for j in range(4):
+        finish(nown, xl * 256, j)
     mirror(0, 1)
+    relay(0, 4)
     own[0].wait()
-    arrived(nrecv, n_r.at[0])
-
-    def block(zz):
-        return pl.ds(pl.multiple_of(zz * 64, 64), 64)
-
-    keep = pl.ds(pl.multiple_of(xl * 256, 256), 256)
-
-    def project(k):
+
+    def project(k, lo, count):
+        at, rows = pl.ds(k * CH, CH), pl.ds(lo, count)
+        total = dot(nown[rows, :], wo_own[:, at]) + dot(nrecv[rows, :], wo_par[:, at])
+        part[rows, at] = total.astype(BF16)
+
+    def far(k):
         ready(0, k)
-
-        def tile(j, carry):
-            at = pl.ds(pl.multiple_of(k * CH + j * 512, 512), 512)
-            total = dot(normed[keep, :], wo_own[:, at]) + dot(nrecv[...], wo_par[:, at])
-            part[:, at] = total.astype(BF16)
-            return carry
-
-        lax.fori_loop(0, CH // 512, tile, 0)
+        project(k, 0, 64)
         left, right = pl.ds(k * CH, HALF), pl.ds(k * CH + HALF, HALF)
         slot = pl.ds(k * HALF, HALF)
-        send(part.at[block(z_far), left], a_p.at[:, slot], a_s.at[k, 0], a_r.at[k, 0], to_zu)
-        send(part.at[block(z_far), right], a_m.at[:, slot], a_s.at[k, 1], a_r.at[k, 1], to_zd)
+        send(part.at[four(0), left], a_p.at[:, slot], a_s.at[k, 0], a_r.at[k, 0], to_zu)
+        send(part.at[four(0), right], a_m.at[:, slot], a_s.at[k, 1], a_r.at[k, 1], to_zd)
 
     def join(k):
         left, right = pl.ds(k * CH, HALF), pl.ds(k * CH + HALF, HALF)
         slot, chunk = pl.ds(k * HALF, HALF), pl.ds(k * CH, CH)
+        project(k, 64, 192)
         arrived(a_p.at[:, slot], a_r.at[k, 0])
-        part[block(z_up), left] = (
-            part[block(z_up), left].astype(F32) + a_p[:, slot].astype(F32)
+        part[four(1), left] = (
+            part[four(1), left].astype(F32) + a_p[:, slot].astype(F32)
         ).astype(BF16)
-        send(part.at[block(z_up), chunk], b_p.at[:, chunk], b_s.at[k, 0], b_r.at[k, 0], to_zu)
+        send(part.at[four(1), chunk], b_p.at[:, chunk], b_s.at[k, 0], b_r.at[k, 0], to_zu)
         arrived(a_m.at[:, slot], a_r.at[k, 1])
-        part[block(z_dn), right] = (
-            part[block(z_dn), right].astype(F32) + a_m[:, slot].astype(F32)
+        part[four(2), right] = (
+            part[four(2), right].astype(F32) + a_m[:, slot].astype(F32)
         ).astype(BF16)
-        send(part.at[block(z_dn), chunk], b_m.at[:, chunk], b_s.at[k, 1], b_r.at[k, 1], to_zd)
+        send(part.at[four(2), chunk], b_m.at[:, chunk], b_s.at[k, 1], b_r.at[k, 1], to_zd)
 
     def close(k):
         chunk = pl.ds(k * CH, CH)
         arrived(b_p.at[:, chunk], b_r.at[k, 0])
         arrived(b_m.at[:, chunk], b_r.at[k, 1])
         total = (
-            residual[:, chunk].astype(F32) + part[block(z), chunk].astype(F32)
+            residual[:, chunk].astype(F32) + part[four(3), chunk].astype(F32)
             + b_p[:, chunk].astype(F32) + b_m[:, chunk].astype(F32)
         )
         upd[:, chunk] = total
         return jnp.sum(total * total, axis=-1, keepdims=True)
 
-    project(0)
+    arrived(nrecv.at[four(0)], n_r.at[0])
+    far(0)
     mirror(0, 2)
-    project(1)
+    far(1)
+    relay(0, 5)
+    for j in range(1, 4):
+        arrived(nrecv.at[four(j)], n_r.at[j])
+    mirror(0, 3)
+    far(2)
     join(0)
-    relay(0, 3)
-    project(2)
+    mirror(0, 4)
+    far(3)
+    relay(0, 6)
     join(1)
-    mirror(0, 3)
-    project(3)
+    mirror(0, 5)
+    far(4)
     join(2)
+    relay(0, 7)
+    mirror(0, 6)
+    far(5)
     join(3)
+    mirror(0, 7)
+    far(6)
+    join(4)
+    far(7)
+    join(5)
+    join(6)
+    join(7)
+    kvbuf[:, :, :, pl.ds(256, HEAD)] = jnp.ones((24, NP, R, HEAD), BF16)
+    own[2].wait()
+    separate(wkv_own, wq_own, 0, MODEL)
     relay(1, 0)
     relay(2, 0)
     square = close(0)
-    square += close(1)
+    for k in range(1, 4):
+        square += close(k)
     relay(1, 1)
     relay(2, 1)
+    square += close(4)
+    square += close(5)
     mirror(1, 0)
     mirror(2, 0)
-    square += close(2)
-    square += close(3)
+    square += close(6)
+    square += close(7)
     scale = lax.rsqrt(square * (1.0 / MODEL) + EPS)
     store = pltpu.make_async_copy(upd, upd_out, own_sem.at[3])
     store.start()
@@ -371,6 +425,7 @@
         arrived(far.at[:, pl.ds(0, MODEL // 2)], g_r.at[p, 2])
         arrived(far.at[:, pl.ds(MODEL // 2, MODEL // 2)], g_r.at[p, 3])
 
+    kv = pl.ds(0, 256)
     mine_half, mine_kv = pl.ds(xl * 4, 4), pl.ds(16 + xl * 4, 4)
 
     def second(p):
@@ -385,38 +440,37 @@
 
         lax.fori_loop(0, 6, deep, 0)
         stkv[p] = acc[:, pl.ds(QKV + 512, 256)].astype(BF16).reshape(4, R, 256)
-        kvbuf[mine_kv, p] = acc[:, pl.ds(512, 256)].astype(BF16).reshape(4, R, 256)
-        send(stkv.at[p], kvbuf.at[mine_kv, p], x_s.at[p, 0], x_r.at[p, 0], to_pair)
+        kvbuf[mine_kv, p, :, kv] = acc[:, pl.ds(512, 256)].astype(BF16).reshape(4, R, 256)
+        send(stkv.at[p], kvbuf.at[mine_kv, p, :, kv], x_s.at[p, 0], x_r.at[p, 0], to_pair)
         for step in (1, 2):
 
             @pl.when(s + step < 16)
             def _(step=step):
-                slot = kvbuf.at[pl.ds(16 - 8 * step + xl * 4, 4), p]
+                slot = kvbuf.at[pl.ds(16 - 8 * step + xl * 4, 4), p, :, kv]
                 sem = h_r.at[p, step - 1, xl]
-                send(kvbuf.at[mine_kv, p], slot, h_s.at[p, step - 1, 0], sem, (s + step, h), False)
+                send(kvbuf.at[mine_kv, p, :, kv], slot, h_s.at[p, step - 1, 0], sem, (s + step, h), False)
                 send(stkv.at[p], slot, h_s.at[p, step - 1, 1], sem, (s + step, other), False)
 
         stq[p] = acc[:, pl.ds(QKV, 512)].astype(BF16).reshape(4, R, 512)
         send(stq.at[p], qbuf.at[mine_half, p], x_s.at[p, 1], x_r.at[p, 1], to_pair)
         qbuf[mine_half, p] = acc[:, pl.ds(0, 512)].astype(BF16).reshape(4, R, 512)
 
-    relay(1, 2)
-    relay(2, 2)
-    mirror(1, 1)
-    mirror(2, 1)
+    for k in (2, 3):
+        relay(1, k)
+        relay(2, k)
+        mirror(1, k - 1)
+        mirror(2, k - 1)
     forward(0)
-    relay(1, 3)
-    relay(2, 3)
-    mirror(1, 2)
-    mirror(2, 2)
-    forward(1)
     mirror(1, 3)
     mirror(2, 3)
+    forward(1)
+    for k in range(4):
+        separate(wkv_par, wq_par, c * 3072 + k * 768, 768)
     own[1].wait()
-    own[2].wait()
     for k in range(4):
         ready(1, k)
         ready(2, k)
+        separate(wkv_par, wq_par, (1 - c) * 3072 + k * 768, 768)
     gathered(0)
     second(0)
     gathered(1)
@@ -424,41 +478,49 @@
 
     @pl.when(s < 1)
     def _():
-        kvbuf[pl.ds(8, 8)] = jnp.zeros((8, NP, R, 256), BF16)
+        kvbuf[pl.ds(8, 8), :, :, kv] = jnp.zeros((8, NP, R, 256), BF16)
 
     @pl.when(s < 2)
     def _():
-        kvbuf[pl.ds(0, 8)] = jnp.zeros((8, NP, R, 256), BF16)
+        kvbuf[pl.ds(0, 8), :, :, kv] = jnp.zeros((8, NP, R, 256), BF16)
 
     for p in range(NP):
-        arrived(kvbuf.at[pl.ds(16 + (1 - xl) * 4, 4), p], x_r.at[p, 0])
+        arrived(kvbuf.at[pl.ds(16 + (1 - xl) * 4, 4), p, :, kv], x_r.at[p, 0])
         for step in (1, 2):
 
             @pl.when(s - step >= 0)
             def _(p=p, step=step):
                 for hf in (0, 1):
-                    slot = kvbuf.at[pl.ds(16 - 8 * step + hf * 4, 4), p]
+                    slot = kvbuf.at[pl.ds(16 - 8 * step + hf * 4, 4), p, :, kv]
                     arrived(slot, h_r.at[p, step - 1, hf])
 
         arrived(qbuf.at[pl.ds((1 - xl) * 4, 4), p], x_r.at[p, 1])
 
+    factor = HEAD**-0.5 * 1.4426950408889634
+
     def attend(t, carry):
-        shape = (HEAD, 1152)
-        row, col = rows_of(shape), cols_of(shape)
-        gap = col - row
+        row, col = rows_of((HEAD, 1)), cols_of((HEAD, 640))
         early = 1024 - s * TOK - t * HEAD
+        middle = cols_of((HEAD, 384)) + 640 >= early
+        last = cols_of((HEAD, HEAD)) <= row
         keys = kvbuf[pl.ds(2 * t, 18), :, :, pl.ds(0, HEAD)].reshape(1152, HEAD)
-        vals = kvbuf[pl.ds(2 * t, 18), :, :, pl.ds(HEAD, HEAD)].reshape(1152, HEAD)
+        vals = kvbuf[pl.ds(2 * t, 18), :, :, pl.ds(HEAD, 256)].reshape(1152, 256)
         for i in range(4):
-            reach = window[h * 4 + i]
-            seen = (gap <= 1024) & (gap > 1024 - reach) & (col >= early)
+            first = jnp.maximum(row + (1025 - window[h * 4 + i]), early)
             q = qbuf[pl.ds(2 * t, 2), :, :, head_of(i)].reshape(HEAD, HEAD)
-            sc = dot_t(q, keys) * (HEAD**-0.5)
-            sc = jnp.where(seen, sc, -1e30)
+            sc = dot_t(q, keys)
+            sc = jnp.concatenate(
+                (
+                    jnp.where(col >= first, sc[:, :640], -1e30),
+                    jnp.where(middle, sc[:, 640:1024], -1e30),
+                    jnp.where(last, sc[:, 1024:], -1e30),
+                ),
+                axis=1,
+            )
             top = jnp.max(sc, axis=-1, keepdims=True)
-            pr = jnp.where(seen, jnp.exp(sc - top), 0.0)
-            total = jnp.sum(pr, axis=-1, keepdims=True)
-            out = dot(pr.astype(BF16), vals) / total
+            pr = jnp.exp2((sc - top) * factor).astype(BF16)
+            both = dot(pr, vals)
+            out = both[:, :HEAD] / both[:, HEAD:]
             att_out[pl.ds(pl.multiple_of(t * HEAD, HEAD), HEAD), head_of(i)] = out.astype(BF16)
         return carry
 
@@ -511,13 +573,17 @@
             V((512, MODEL), BF16),
             V((MODEL, QKV), BF16),
             V((MODEL, QKV), BF16),
+            V((2 * MODEL, HEAD), BF16),
+            V((2 * MODEL, HEAD), BF16),
+            V((768, HEAD), F32),
             V((4, HEAD, HEAD), F32),
             V((4, HEAD, HEAD), F32),
             V((2, HEAD, HEAD), BF16),
             V((7, 2, HEAD, HEAD), BF16),
             V((4, HEAD, HEAD), F32),
             V((TOK, 512), F32),
-            V((TOK, 512), BF16),
+            V((256, 512), BF16),
+            V((256, 512), BF16),
             V((256, 512), BF16),
             V((256, MODEL), BF16),
             V((64, MODEL // 2), BF16),
@@ -528,18 +594,18 @@
             V((NP, 4, R, MODEL), BF16),
             V((4 * R, 2 * QKV), F32),
             V((8, NP, R, 512), BF16),
-            V((24, NP, R, 256), BF16),
+            V((24, NP, R, 384), BF16),
             V((NP, 4, R, 512), BF16),
             V((NP, 4, R, 256), BF16),
             dma((4,)),
-            dma((3, 4, 5)),
-            dma((3, 4, 5)),
+            dma((3, NCH, 5)),
+            dma((3, NCH, 5)),
             dma((2,)),
             dma((2,)),
             dma((7,)),
             dma((7,)),
-            dma((1,)),
-            dma((1,)),
+            dma((4,)),
+            dma((4,)),
             dma((NCH, 2)),
             dma((NCH, 2)),
             dma((NCH, 2)),
@@ -562,7 +628,7 @@
         out_weight,
         attn_gain.reshape(1, MODEL),
         query_weight,
-        key_value_weight.reshape(MODEL, 256),
+        key_value_weight.reshape(2 * MODEL, HEAD),
         window,
     )
 

time: 128 us -> 116 us (0.906); the launches traced: 128 us -> 114 us
  Pallas kernels: 120 us -> 110 us
  local copies, waits for them, and re-layouts: 7.47 us -> 3.52 us
    pallas_call x1, Pallas kernels: 120 us -> 110 us  [on_device(): pl.pallas_call(body, out_shape=(jax.ShapeDtypeStruct((64, MODEL), F32), j...]
    unnamed x5 -> x4, local copies, waits for them, and re-layouts: 7.47 us -> 3.52 us
where the time goes in v2:
time: 116 us; the launch traced here: 114 us
  Pallas kernels  110 us (95%)
  local copies, waits for them, and re-layouts  3.52 us (3%)
    pallas_call x1, Pallas kernels, on_device(): pl.pallas_call(body, out_shape=(jax.ShapeDtypeStruct((64, MODEL), F32), j...  110 us
    unnamed x4, local copies, waits for them, and re-layouts  3.52 us

profile of v2, /device:TPU:1, one launch (start us, length us, event | category | flops | bytes accessed | tf_op | source)
XLA Modules:
  0.0 114.4 jit_solution(5717136524233339687)
XLA Ops:
  0.6 110.2 %shard_map.104 = (f32[64,6144]{1,0:T(8,128)}, bf16[512,512]{1,0:T(8,128)(2,1)}) custom-call(bf16[3,512,512]{2,1,0:T(8,128)(2,1)} %bitcast.5, bf16[64,6144]{1,0:T(8,128)(2,1)} %residual.1, f32[32]{0:T(128)} %decay.1, f32[1,512]{1,0:T(1,128)} %bitcast.7, bf16[512,6144]{1,0:T(8,128)(2,1)} %wo_hbm.1, f32[1,6144]{1,0:T(1,128)} %bitcast.6, ...), custom_call_target="tpu_custom_call" | custom-call | tf_op jit(solution)/shard_map/pallas_call | solution.py:563
  110.9 0.0 copy-start
  110.9 2.7 %copy.13 = f32[64,6144]{1,0:T(8,128)} copy(f32[64,6144]{1,0:T(8,128)} %get-tuple-element.4) | data formatting | bytes 3145728
  113.6 0.0 copy-done
  113.6 0.8 copy.14
Async XLA Ops:
  110.9 2.7 %copy-start = (bf16[512,512]{1,0:T(8,128)(2,1)S(1)}, bf16[512,512]{1,0:T(8,128)(2,1)}, u32[]{:S(2)}) copy-start(bf16[512,512]{1,0:T(8,128)(2,1)} %get-tuple-element.5) | copy-start | bytes 1572868

commit v3 on v2

--- a/solution.py
+++ b/solution.py
@@ -83,6 +83,7 @@
     b_m,
     upd,
     gath,
+    scales,
     acc,
     qbuf,
     kvbuf,
@@ -103,6 +104,8 @@
     b_r,
     g_s,
     g_r,
+    l_s,
+    l_r,
     x_s,
     x_r,
     h_s,
@@ -321,38 +324,33 @@
     def project(k, lo, count):
         at, rows = pl.ds(k * CH, CH), pl.ds(lo, count)
         total = dot(nown[rows, :], wo_own[:, at]) + dot(nrecv[rows, :], wo_par[:, at])
-        part[rows, at] = total.astype(BF16)
+        part[k, rows] = total.astype(BF16)
+
+    low, high = pl.ds(0, 32), pl.ds(32, 32)
 
     def far(k):
         ready(0, k)
         project(k, 0, 64)
-        left, right = pl.ds(k * CH, HALF), pl.ds(k * CH + HALF, HALF)
-        slot = pl.ds(k * HALF, HALF)
-        send(part.at[four(0), left], a_p.at[:, slot], a_s.at[k, 0], a_r.at[k, 0], to_zu)
-        send(part.at[four(0), right], a_m.at[:, slot], a_s.at[k, 1], a_r.at[k, 1], to_zd)
+        send(part.at[k, low], a_p.at[k], a_s.at[k, 0], a_r.at[k, 0], to_zu)
+        send(part.at[k, high], a_m.at[k], a_s.at[k, 1], a_r.at[k, 1], to_zd)
 
     def join(k):
-        left, right = pl.ds(k * CH, HALF), pl.ds(k * CH + HALF, HALF)
-        slot, chunk = pl.ds(k * HALF, HALF), pl.ds(k * CH, CH)
         project(k, 64, 192)
-        arrived(a_p.at[:, slot], a_r.at[k, 0])
-        part[four(1), left] = (
-            part[four(1), left].astype(F32) + a_p[:, slot].astype(F32)
-        ).astype(BF16)
-        send(part.at[four(1), chunk], b_p.at[:, chunk], b_s.at[k, 0], b_r.at[k, 0], to_zu)
-        arrived(a_m.at[:, slot], a_r.at[k, 1])
-        part[four(2), right] = (
-            part[four(2), right].astype(F32) + a_m[:, slot].astype(F32)
-        ).astype(BF16)
-        send(part.at[four(2), chunk], b_m.at[:, chunk], b_s.at[k, 1], b_r.at[k, 1], to_zd)
+        one, two = pl.ds(64, 32), pl.ds(160, 32)
+        arrived(a_p.at[k], a_r.at[k, 0])
+        part[k, one] = (part[k, one].astype(F32) + a_p[k].astype(F32)).astype(BF16)
+        send(part.at[k, four(1)], b_p.at[k], b_s.at[k, 0], b_r.at[k, 0], to_zu)
+        arrived(a_m.at[k], a_r.at[k, 1])
+        part[k, two] = (part[k, two].astype(F32) + a_m[k].astype(F32)).astype(BF16)
+        send(part.at[k, four(2)], b_m.at[k], b_s.at[k, 1], b_r.at[k, 1], to_zd)
 
     def close(k):
         chunk = pl.ds(k * CH, CH)
-        arrived(b_p.at[:, chunk], b_r.at[k, 0])
-        arrived(b_m.at[:, chunk], b_r.at[k, 1])
+        arrived(b_p.at[k], b_r.at[k, 0])
+        arrived(b_m.at[k], b_r.at[k, 1])
         total = (
-            residual[:, chunk].astype(F32) + part[four(3), chunk].astype(F32)
-            + b_p[:, chunk].astype(F32) + b_m[:, chunk].astype(F32)
+            residual[:, chunk].astype(F32) + part[k, four(3)].astype(F32)
+            + b_p[k].astype(F32) + b_m[k].astype(F32)
         )
         upd[:, chunk] = total
         return jnp.sum(total * total, axis=-1, keepdims=True)
@@ -388,57 +386,83 @@
     kvbuf[:, :, :, pl.ds(256, HEAD)] = jnp.ones((24, NP, R, HEAD), BF16)
     own[2].wait()
     separate(wkv_own, wq_own, 0, MODEL)
-    relay(1, 0)
-    relay(2, 0)
     square = close(0)
     for k in range(1, 4):
         square += close(k)
+
+    first_rows, wide_half = pl.ds(0, R), MODEL // 2
+
+    def early(i):
+        cols = pl.ds(i * wide_half, wide_half)
+        gath[0, z, :, cols] = (upd[first_rows, cols] * again[:, cols]).astype(BF16)
+        mine = gath.at[0, z, :, cols]
+        send(mine, mine, g_s.at[0, 2 * i], g_r.at[0, 2 * i], to_zu)
+        send(mine, mine, g_s.at[0, 2 * i + 1], g_r.at[0, 2 * i + 1], to_zd)
+
+    early(0)
+    relay(1, 0)
+    relay(2, 0)
+    square += close(4)
+    square += close(5)
+    square += close(6)
+    square += close(7)
+    early(1)
+    scale = lax.rsqrt(square * (1.0 / MODEL) + EPS)
+    scales[z] = jnp.broadcast_to(scale[:R], (R, HEAD))
+    for i, target in enumerate((to_zu, to_zd, place(x, y, c, z + 2))):
+        send(scales.at[z], scales.at[z], l_s.at[i], l_r.at[i], target)
+    row = pl.ds(R, R)
+    gath[1, z] = (upd[row, :] * scale[R:] * again[...]).astype(BF16)
+    mine = gath.at[1, z]
+    send(mine, mine, g_s.at[1, 0], g_r.at[1, 0], to_zu)
+    send(mine, mine, g_s.at[1, 1], g_r.at[1, 1], to_zd)
+    store = pltpu.make_async_copy(upd, upd_out, own_sem.at[3])
+    store.start()
     relay(1, 1)
     relay(2, 1)
-    square += close(4)
-    square += close(5)
     mirror(1, 0)
     mirror(2, 0)
-    square += close(6)
-    square += close(7)
-    scale = lax.rsqrt(square * (1.0 / MODEL) + EPS)
-    store = pltpu.make_async_copy(upd, upd_out, own_sem.at[3])
-    store.start()
-
-    for p in range(NP):
-        row = pl.ds(p * R, R)
-        gath[p, z] = (upd[row, :] * scale[p * R : (p + 1) * R] * again[...]).astype(BF16)
-        mine = gath.at[p, z]
-        send(mine, mine, g_s.at[p, 0], g_r.at[p, 0], to_zu)
-        send(mine, mine, g_s.at[p, 1], g_r.at[p, 1], to_zd)
+
+    up_rows, dn_rows = pl.ds(0, R // 2), pl.ds(R // 2, R // 2)
 
     def forward(p):
         below, above = gath.at[p, z_dn], gath.at[p, z_up]
-        left, right = pl.ds(0, MODEL // 2), pl.ds(MODEL // 2, MODEL // 2)
-        arrived(below, g_r.at[p, 0])
-        send(below.at[:, left], below.at[:, left], g_s.at[p, 2], g_r.at[p, 2], to_zu)
-        arrived(above, g_r.at[p, 1])
-        send(above.at[:, right], above.at[:, right], g_s.at[p, 3], g_r.at[p, 3], to_zd)
+        for d, block in ((0, below), (1, above)):
+            if p == 0:
+                for i in (0, 1):
+                    arrived(block.at[:, pl.ds(i * wide_half, wide_half)], g_r.at[0, 2 * i + d])
+            else:
+                arrived(block, g_r.at[p, d])
+            half = block.at[(up_rows, dn_rows)[d]]
+            send(half, half, g_s.at[p, 4 + d], g_r.at[p, 4 + d], (to_zu, to_zd)[d])
 
     def gathered(p):
-        far = gath.at[p, z_far]
-        arrived(far.at[:, pl.ds(0, MODEL // 2)], g_r.at[p, 2])
-        arrived(far.at[:, pl.ds(MODEL // 2, MODEL // 2)], g_r.at[p, 3])
+        arrived(gath.at[p, z_far, up_rows], g_r.at[p, 4])
+        arrived(gath.at[p, z_far, dn_rows], g_r.at[p, 5])
+        if p == 0:
+            for i, there in enumerate((z_dn, z_up, z_far)):
+                arrived(scales.at[there], l_r.at[i])
 
     kv = pl.ds(0, 256)
     mine_half, mine_kv = pl.ds(xl * 4, 4), pl.ds(16 + xl * 4, 4)
 
     def second(p):
-        acc[...] = jnp.zeros_like(acc)
-
-        def deep(j, carry):
-            at = pl.ds(pl.multiple_of(j * 1024, 1024), 1024)
-            lhs = gath[p, :, :, at].reshape(4 * R, 1024)
-            acc[:, pl.ds(0, QKV)] += dot(lhs, wq_own[at, :])
-            acc[:, pl.ds(QKV, QKV)] += dot(lhs, wq_par[at, :])
-            return carry
-
-        lax.fori_loop(0, 6, deep, 0)
+        def product(weight, first, count, to):
+            out = pl.ds(to, count)
+            acc[:, out] = jnp.zeros((4 * R, count), F32)
+
+            def deep(j, carry):
+                at = pl.ds(pl.multiple_of(j * 1024, 1024), 1024)
+                lhs = gath[p, :, :, at].reshape(4 * R, 1024)
+                acc[:, out] += dot(lhs, weight[at, pl.ds(first, count)])
+                return carry
+
+            lax.fori_loop(0, 6, deep, 0)
+            if p == 0:
+                acc[:, out] *= scales[...].reshape(4 * R, HEAD)[:, :1]
+
+        product(wq_par, 512, 256, QKV + 512)
+        product(wq_own, 512, 256, 512)
         stkv[p] = acc[:, pl.ds(QKV + 512, 256)].astype(BF16).reshape(4, R, 256)
         kvbuf[mine_kv, p, :, kv] = acc[:, pl.ds(512, 256)].astype(BF16).reshape(4, R, 256)
         send(stkv.at[p], kvbuf.at[mine_kv, p, :, kv], x_s.at[p, 0], x_r.at[p, 0], to_pair)
@@ -451,8 +475,10 @@
                 send(kvbuf.at[mine_kv, p, :, kv], slot, h_s.at[p, step - 1, 0], sem, (s + step, h), False)
                 send(stkv.at[p], slot, h_s.at[p, step - 1, 1], sem, (s + step, other), False)
 
+        product(wq_par, 0, 512, QKV)
         stq[p] = acc[:, pl.ds(QKV, 512)].astype(BF16).reshape(4, R, 512)
         send(stq.at[p], qbuf.at[mine_half, p], x_s.at[p, 1], x_r.at[p, 1], to_pair)
+        product(wq_own, 0, 512, 0)
         qbuf[mine_half, p] = acc[:, pl.ds(0, 512)].astype(BF16).reshape(4, R, 512)
 
     for k in (2, 3):
@@ -585,13 +611,14 @@
             V((256, 512), BF16),
             V((256, 512), BF16),
             V((256, 512), BF16),
-            V((256, MODEL), BF16),
-            V((64, MODEL // 2), BF16),
-            V((64, MODEL // 2), BF16),
-            V((64, MODEL), BF16),
-            V((64, MODEL), BF16),
+            V((NCH, 256, CH), BF16),
+            V((NCH, 32, CH), BF16),
+            V((NCH, 32, CH), BF16),
+            V((NCH, 64, CH), BF16),
+            V((NCH, 64, CH), BF16),
             V((64, MODEL), F32),
             V((NP, 4, R, MODEL), BF16),
+            V((4, R, HEAD), F32),
             V((4 * R, 2 * QKV), F32),
             V((8, NP, R, 512), BF16),
             V((24, NP, R, 384), BF16),
@@ -610,8 +637,10 @@
             dma((NCH, 2)),
             dma((NCH, 2)),
             dma((NCH, 2)),
-            dma((NP, 4)),
-            dma((NP, 4)),
+            dma((NP, 6)),
+            dma((NP, 6)),
+            dma((3,)),
+            dma((3,)),
             dma((NP, 2)),
             dma((NP, 2)),
             dma((NP, 2, 2)),

time: 116 us -> 117 us (level); the launches traced: 114 us -> 117 us
  Pallas kernels: 110 us -> 113 us
    pallas_call x1, Pallas kernels: 110 us -> 113 us  [on_device(): pl.pallas_call(body, out_shape=(jax.ShapeDtypeStruct((64, MODEL), F32), j...]
where the time goes in v3:
time: 117 us
  Pallas kernels  113 us (97%)
  local copies, waits for them, and re-layouts  3.52 us (3%)
    pallas_call x1, Pallas kernels, on_device(): pl.pallas_call(body, out_shape=(jax.ShapeDtypeStruct((64, MODEL), F32), j...  113 us
    unnamed x4, local copies, waits for them, and re-layouts  3.52 us

profile of v3, /device:TPU:1, one launch (start us, length us, event | category | flops | bytes accessed | tf_op | source)
XLA Modules:
  0.0 116.7 jit_solution(4904848837135147567)
XLA Ops:
  0.6 112.5 %shard_map.104 = (f32[64,6144]{1,0:T(8,128)}, bf16[512,512]{1,0:T(8,128)(2,1)}) custom-call(bf16[3,512,512]{2,1,0:T(8,128)(2,1)} %bitcast.5, bf16[64,6144]{1,0:T(8,128)(2,1)} %residual.1, f32[32]{0:T(128)} %decay.1, f32[1,512]{1,0:T(1,128)} %bitcast.7, bf16[512,6144]{1,0:T(8,128)(2,1)} %wo_hbm.1, f32[1,6144]{1,0:T(1,128)} %bitcast.6, ...), custom_call_target="tpu_custom_call" | custom-call | tf_op jit(solution)/shard_map/pallas_call | solution.py:589
  113.2 0.0 copy-start
  113.2 2.7 %copy.13 = f32[64,6144]{1,0:T(8,128)} copy(f32[64,6144]{1,0:T(8,128)} %get-tuple-element.4) | data formatting | bytes 3145728
  115.9 0.0 copy-done
  115.9 0.8 copy.14
Async XLA Ops:
  113.2 2.7 %copy-start = (bf16[512,512]{1,0:T(8,128)(2,1)S(1)}, bf16[512,512]{1,0:T(8,128)(2,1)}, u32[]{:S(2)}) copy-start(bf16[512,512]{1,0:T(8,128)(2,1)} %get-tuple-element.5) | copy-start | bytes 1572868

commit v4 on v2

--- a/solution.py
+++ b/solution.py
@@ -274,7 +274,6 @@
 
     half_p = p_all.at[pl.ds(2 * c, 2)]
     across = send(half_p, half_p, sp_s.at[1], sp_r.at[1], to_core, False)
-    relay(0, 2)
     arrived(p_all.at[pl.ds(2 * (1 - c), 2)], sp_r.at[1])
 
     order = (z_far, z_up, z_dn, z)
@@ -310,12 +309,11 @@
     for k in range(4):
         push(1, k, 0)
         push(2, k, 0)
-    relay(0, 3)
-    mirror(0, 0)
+    relay(0, 2)
     for j in range(4):
         finish(nown, xl * 256, j)
-    mirror(0, 1)
-    relay(0, 4)
+    mirror(0, 0)
+    relay(0, 3)
     own[0].wait()
 
     def project(k, lo, count):
@@ -359,30 +357,32 @@
 
     arrived(nrecv.at[four(0)], n_r.at[0])
     far(0)
-    mirror(0, 2)
+    mirror(0, 1)
     far(1)
-    relay(0, 5)
+    relay(0, 4)
     for j in range(1, 4):
         arrived(nrecv.at[four(j)], n_r.at[j])
+    join(0)
+    mirror(0, 2)
+    far(2)
+    relay(0, 5)
+    join(1)
     mirror(0, 3)
-    far(2)
-    join(0)
-    mirror(0, 4)
     far(3)
     relay(0, 6)
-    join(1)
+    join(2)
+    mirror(0, 4)
+    far(4)
+    relay(0, 7)
+    join(3)
     mirror(0, 5)
-    far(4)
-    join(2)
-    relay(0, 7)
+    far(5)
+    join(4)
     mirror(0, 6)
-    far(5)
-    join(3)
+    far(6)
+    join(5)
     mirror(0, 7)
-    far(6)
-    join(4)
     far(7)
-    join(5)
     join(6)
     join(7)
     kvbuf[:, :, :, pl.ds(256, HEAD)] = jnp.ones((24, NP, R, HEAD), BF16)

time: 116 us -> 120 us (1.034)
  Pallas kernels: 110 us -> 114 us
    pallas_call x1, Pallas kernels: 110 us -> 114 us  [on_device(): pl.pallas_call(body, out_shape=(jax.ShapeDtypeStruct((64, MODEL), F32), j...]
where the time goes in v4:
time: 120 us; the launch traced here: 118 us
  Pallas kernels  114 us (95%)
  local copies, waits for them, and re-layouts  3.52 us (3%)
    pallas_call x1, Pallas kernels, on_device(): pl.pallas_call(body, out_shape=(jax.ShapeDtypeStruct((64, MODEL), F32), j...  114 us
    unnamed x4, local copies, waits for them, and re-layouts  3.52 us

profile of v4, /device:TPU:1, one launch (start us, length us, event | category | flops | bytes accessed | tf_op | source)
XLA Modules:
  0.0 118.3 jit_solution(6212511686215139406)
XLA Ops:
  0.6 114.1 %shard_map.104 = (f32[64,6144]{1,0:T(8,128)}, bf16[512,512]{1,0:T(8,128)(2,1)}) custom-call(bf16[3,512,512]{2,1,0:T(8,128)(2,1)} %bitcast.5, bf16[64,6144]{1,0:T(8,128)(2,1)} %residual.1, f32[32]{0:T(128)} %decay.1, f32[1,512]{1,0:T(1,128)} %bitcast.7, bf16[512,6144]{1,0:T(8,128)(2,1)} %wo_hbm.1, f32[1,6144]{1,0:T(1,128)} %bitcast.6, ...), custom_call_target="tpu_custom_call" | custom-call | tf_op jit(solution)/shard_map/pallas_call | solution.py:563
  114.8 0.0 copy-start
  114.8 2.7 %copy.13 = f32[64,6144]{1,0:T(8,128)} copy(f32[64,6144]{1,0:T(8,128)} %get-tuple-element.4) | data formatting | bytes 3145728
  117.5 0.0 copy-done
  117.5 0.8 copy.14
Async XLA Ops:
  114.8 2.7 %copy-start = (bf16[512,512]{1,0:T(8,128)(2,1)S(1)}, bf16[512,512]{1,0:T(8,128)(2,1)}, u32[]{:S(2)}) copy-start(bf16[512,512]{1,0:T(8,128)(2,1)} %get-tuple-element.5) | copy-start | bytes 1572868
